TPU v7x, 256 devices: a whole 4x4x8 slice. The times are simulated.
256 devices in a mesh: cube: 8 (over z), row: 4 (over y_lo, core), col: 8 (over y_hi, x).
Axes of the slice: x: 4, y: 4 (y_hi: 2, y_lo: 2; y = y_hi * 2 + y_lo), z: 8, core: 2. Of those that a mesh axis runs over, the one named last changes fastest.
Arguments:
- diag_block: float32 [8, 256, 256], P('cube', ('row', 'col'))
- pivot_order: int32 [8, 256], P('cube'), may hold values from 0 to 255, as said below
- lower_in: bfloat16 [8, 4096, 256], P('cube', 'row', 'col'), may hold values from -0.14941406 to 0.14941406
- upper_in: bfloat16 [8, 256, 30720], P('cube', 'row', 'col'), may hold values from -6 to 6
- trailing: bfloat16 [8, 4096, 30720], P('cube', 'row', 'col'), may hold values from -6 to 6
- block_mask: int32 [8, 32, 16], P('cube', 'row', 'col'), may hold values 0 or 1
- row_map: int32 [8, 4096], P('cube', 'row'), may hold values from 0 to 1023, as said below
Outputs:
- merged: bfloat16 [8, 4096, 15360], P('cube', 'row', 'col')
Inputs may be any that keep to these rules, and one draw needn't show every extreme that they name: `pivot_order`: each front's row is a permutation of 0 to 255. `row_map`: in each aligned block of 1024 rows of a front the entries are a permutation of 0 to 1023.
All inputs are finite; a program needn't handle non-finite values. No bound on the sum of `block_mask` on one device may be relied on, other than what follows from the above.
Results may differ from a plain program's by a relative error of at most 0.0056.
Values may be sent and summed in bfloat16 or wider, within the bound.
A program may use at most 192 MiB of HBM per device.

v0:
```python
import functools

import jax
import jax.numpy as jnp
from jax import lax
from jax.experimental import pallas as pl
from jax.experimental.pallas import tpu as pltpu
from jax.sharding import PartitionSpec as P

MESH = pl.DeviceIdType.MESH
RAW = (384, 384, 384)
COOKED = (384, 256, 128)
STEP = 64


def offsets(widths, start):
    spans = []
    for width in widths:
        spans.append((start, width))
        start += width
    return spans


def invert(amat):
    size = amat.shape[0]
    lane = lax.broadcasted_iota(jnp.int32, (1, size), 1)
    sub = lax.broadcasted_iota(jnp.int32, (STEP, 1), 0)

    def block_step(_, carry):
        x = amat[0:STEP, :]
        for k in range(STEP):
            column = jnp.broadcast_to(x[:, k : k + 1], (STEP, size))
            here = lane == k
            inverse = 1.0 / column[k : k + 1, :]
            fresh = jnp.where(here, inverse, x[k : k + 1, :] * inverse)
            x = jnp.where(sub == k, fresh, jnp.where(here, 0.0, x) - column * fresh)
        below = amat[STEP:, :]
        rest = jnp.where(lane < STEP, 0.0, below) - jnp.dot(
            below[:, 0:STEP],
            x,
            precision=lax.Precision.HIGHEST,
            preferred_element_type=jnp.float32,
        )
        amat[0 : size - STEP, :] = jnp.concatenate([rest[:, STEP:], rest[:, :STEP]], axis=1)
        amat[size - STEP :, :] = jnp.concatenate([x[:, STEP:], x[:, :STEP]], axis=1)
        return carry

    lax.fori_loop(0, size // STEP, block_step, 0)


def update(block, spans_from, panel, right, right_from, width):
    rows = 256

    def body(step, carry):
        top = pl.multiple_of(step * rows, rows)
        product = jnp.dot(
            panel[pl.ds(top, rows), :],
            right[:, pl.ds(right_from, width)],
            preferred_element_type=jnp.float32,
        )
        where = (pl.ds(top, rows), pl.ds(spans_from, width))
        block[where] = (block[where].astype(jnp.float32) - product).astype(jnp.bfloat16)
        return carry

    lax.fori_loop(0, block.shape[0] // rows, body, 0)


def kernel(
    diag, order_s, order_v, lower, upper, trailing, mask, row_map, out,
    dg, lt, u, ug, land, keep, cook, amat, wk, ws, wo, wg, mo, mg, perm,
    d_send, d_recv, l_send, l_recv, u_send, u_recv, f_send, f_recv,
    v_send, v_recv, z_send, z_recv, local_sem, out_sem,
):
    n_row, n_col = lax.axis_size("row"), lax.axis_size("col")
    c, r, q = lax.axis_index("cube"), lax.axis_index("row"), lax.axis_index("col")
    parity = lax.rem(c, 2)
    peer = (c + 1 - 2 * parity, r, q)
    row_mates = [(c, lax.rem(r + d, n_row), q) for d in range(1, n_row)]
    col_mates = [(c, r, lax.rem(q + d, n_col)) for d in range(1, n_col)]

    m_dev = keep.shape[0]
    half = keep.shape[1]
    raw_width = ug.shape[1]
    kept_at = pl.multiple_of(parity * half, 128)
    sent_at = pl.multiple_of((1 - parity) * half, 128)
    raw_spans = offsets(RAW, 0)
    cooked_spans = offsets(COOKED, raw_width)

    def remote(src, dst, send, recv, to):
        return pltpu.make_async_remote_copy(
            src_ref=src, dst_ref=dst, send_sem=send, recv_sem=recv,
            device_id=to, device_id_type=MESH,
        )

    barrier = pltpu.get_barrier_semaphore()
    for mate in [peer] + row_mates + col_mates:
        pl.semaphore_signal(barrier, inc=1, device_id=mate, device_id_type=MESH)
    pl.semaphore_wait(barrier, n_row + n_col - 1)

    d_rows = diag.shape[1]
    d_at = pl.multiple_of(q * d_rows, d_rows)
    u_rows = upper.shape[1]
    u_at = pl.multiple_of(r * u_rows, u_rows)
    l_rows = lower.shape[1]
    l_at = pl.multiple_of(q * l_rows, l_rows)
    w_rows = m_dev // n_col
    w_at = pl.multiple_of(q * w_rows, w_rows)

    d_own = pltpu.make_async_copy(diag.at[0], dg.at[r, pl.ds(d_at, d_rows), :], local_sem.at[0])
    d_own.start()
    d_first = []
    for i, mate in enumerate(row_mates):
        copy = remote(diag.at[0], dg.at[r, pl.ds(d_at, d_rows), :], d_send.at[i], d_recv.at[i], mate)
        copy.start()
        d_first.append(copy)

    for i in range(mo.shape[0]):
        flag = mask[0, 1 - parity, i].astype(jnp.float32)
        mo[i : i + 1, :] = jnp.full((1, mo.shape[1]), flag, jnp.float32)
    z_copies = []

    def to_peer(src, dst):
        i = len(z_copies)
        copy = remote(src, dst, z_send.at[i], z_recv.at[i], peer)
        copy.start()
        z_copies.append(copy)
        return copy

    m_raw = to_peer(mo, mg)
    u_raw = to_peer(
        upper.at[0, :, pl.ds(sent_at, raw_width)], ug.at[pl.ds(u_at, u_rows), :]
    )
    raw = [
        to_peer(trailing.at[0, :, pl.ds(sent_at + at, width)], land.at[:, pl.ds(at, width)])
        for at, width in raw_spans
    ]

    d_own.wait()
    for copy in d_first:
        copy.wait_recv()
    d_second = []
    for i, mate in enumerate(col_mates):
        part = dg.at[:, pl.ds(d_at, d_rows), :]
        copy = remote(part, part, d_send.at[n_row - 1 + i], d_recv.at[n_row - 1 + i], mate)
        copy.start()
        d_second.append(copy)

    l_own = pltpu.make_async_copy(lower.at[0], lt.at[pl.ds(l_at, l_rows), :], local_sem.at[1])
    l_own.start()
    l_copies = []
    for i, mate in enumerate(col_mates):
        copy = remote(lower.at[0], lt.at[pl.ds(l_at, l_rows), :], l_send.at[i], l_recv.at[i], mate)
        copy.start()
        l_copies.append(copy)
    u_own = pltpu.make_async_copy(upper.at[0], u.at[pl.ds(u_at, u_rows), :], local_sem.at[2])
    u_own.start()
    u_copies = []
    for i, mate in enumerate(row_mates):
        copy = remote(upper.at[0], u.at[pl.ds(u_at, u_rows), :], u_send.at[i], u_recv.at[i], mate)
        copy.start()
        u_copies.append(copy)
    cook_in = pltpu.make_async_copy(
        trailing.at[0, :, pl.ds(sent_at + raw_width, half - raw_width)], cook, local_sem.at[3]
    )
    cook_in.start()
    keep_in = pltpu.make_async_copy(
        trailing.at[0, :, pl.ds(kept_at, half)], keep, local_sem.at[4]
    )
    keep_in.start()

    tile = 128
    lane = lax.broadcasted_iota(jnp.int32, (tile, tile), 1)
    for i in range(m_dev // tile):
        along = jnp.broadcast_to(row_map[:, i * tile : (i + 1) * tile], (tile, tile))
        target = along.astype(jnp.float32).T.astype(jnp.int32)
        for j in range(m_dev // tile):
            hit = jnp.where(lane + j * tile == target, 1.0, 0.0)
            perm[i * tile : (i + 1) * tile, j * tile : (j + 1) * tile] = hit.astype(jnp.bfloat16)

    for copy in d_second:
        copy.wait_recv()
    size = amat.shape[0]
    per_row = dg.shape[1]

    def pick(i, carry):
        source = order_s[0, i]
        amat[pl.ds(i, 1), :] = dg[source // per_row, pl.ds(source % per_row, 1), :]
        return carry

    lax.fori_loop(0, size, pick, 0)
    invert(amat)

    u_raw.wait_recv()
    u_pass = []
    for i, mate in enumerate(row_mates):
        part = ug.at[pl.ds(u_at, u_rows), :]
        copy = remote(part, part, f_send.at[i], f_recv.at[i], mate)
        copy.start()
        u_pass.append(copy)

    xt = amat[...].T
    high = xt.astype(jnp.bfloat16)
    left = xt - high.astype(jnp.float32)
    middle = left.astype(jnp.bfloat16)
    low = (left - middle.astype(jnp.float32)).astype(jnp.bfloat16)
    subs = lax.broadcasted_iota(jnp.int32, (size, size), 0)
    hot = jnp.where(subs == order_v[...], 1.0, 0.0).astype(jnp.bfloat16)
    l_own.wait()
    for copy in l_copies:
        copy.wait_recv()

    def panel(i, carry):
        at = pl.multiple_of(i * tile, tile)
        part = lt[:, pl.ds(at, tile)]
        wt = (
            jnp.dot(low, part, preferred_element_type=jnp.float32)
            + jnp.dot(middle, part, preferred_element_type=jnp.float32)
            + jnp.dot(high, part, preferred_element_type=jnp.float32)
        )
        w = jnp.dot(hot, wt.astype(jnp.bfloat16), preferred_element_type=jnp.float32).T
        wk[pl.ds(at, tile), :] = (w * mask[0, parity, i].astype(jnp.float32)).astype(jnp.bfloat16)
        ws[pl.ds(at, tile), :] = (w * mask[0, 1 - parity, i].astype(jnp.float32)).astype(jnp.bfloat16)
        wo[pl.ds(at, tile), :] = w.astype(jnp.bfloat16)
        return carry

    lax.fori_loop(0, m_dev // tile, panel, 0)
    w_raw = to_peer(wo.at[pl.ds(w_at, w_rows), :], wg.at[pl.ds(w_at, w_rows), :])

    u_own.wait()
    for copy in u_copies:
        copy.wait_recv()
    cook_in.wait()
    cooked = []
    for at, width in cooked_spans:
        start = at - raw_width
        update(cook, start, ws, u, sent_at + at, width)
        cooked.append(to_peer(cook.at[:, pl.ds(start, width)], land.at[:, pl.ds(at, width)]))

    keep_in.wait()
    for at in range(0, half, 384):
        update(keep, at, wk, u, kept_at + at, 384)

    w_raw.wait_recv()
    w_pass = []
    for i, mate in enumerate(col_mates):
        part = wg.at[pl.ds(w_at, w_rows), :]
        copy = remote(part, part, v_send.at[i], v_recv.at[i], mate)
        copy.start()
        w_pass.append(copy)
    for copy in [m_raw] + u_pass + w_pass:
        copy.wait_recv()
    for i in range(mg.shape[0]):
        block = slice(i * tile, (i + 1) * tile)
        masked = wg[block, :].astype(jnp.float32) * mg[i : i + 1, :]
        ws[block, :] = masked.astype(jnp.bfloat16)

    def merge(at, width):
        rows = 256

        def body(step, carry):
            top = pl.multiple_of(step * rows, rows)
            taken = jnp.dot(
                perm[pl.ds(top, rows), :],
                land[:, at : at + width],
                preferred_element_type=jnp.float32,
            )
            where = (pl.ds(top, rows), pl.ds(at, width))
            keep[where] = (keep[where].astype(jnp.float32) + taken).astype(jnp.bfloat16)
            return carry

        lax.fori_loop(0, m_dev // rows, body, 0)

    outs = []

    def write(at, width):
        i = len(outs)
        copy = pltpu.make_async_copy(
            keep.at[:, pl.ds(at, width)], out.at[0, :, pl.ds(at, width)], out_sem.at[i]
        )
        copy.start()
        outs.append(copy)

    for (at, width), copy in zip(raw_spans, raw):
        copy.wait_recv()
        update(land, at, ws, ug, at, width)
        merge(at, width)
        write(at, width)
    for (at, width), copy in zip(cooked_spans, cooked):
        copy.wait_recv()
        merge(at, width)
        write(at, width)

    for copy in d_first + d_second + l_copies + u_copies + u_pass + w_pass + z_copies:
        copy.wait_send()
    for copy in outs:
        copy.wait()


def local(diag_block, pivot_order, lower_in, upper_in, trailing, block_mask, row_map):
    n_row, n_col = lax.axis_size("row"), lax.axis_size("col")
    size = diag_block.shape[2]
    m_dev, wide = trailing.shape[1:]
    half = wide // 2
    raw_width = sum(RAW)
    n_z = 3 + len(RAW) + len(COOKED)
    dma = pltpu.SemaphoreType.DMA
    bf16, f32 = jnp.bfloat16, jnp.float32
    hbm = pl.BlockSpec(memory_space=pl.ANY)
    vmem = pl.BlockSpec(memory_space=pltpu.VMEM)
    smem = pl.BlockSpec(memory_space=pltpu.SMEM)
    return pl.pallas_call(
        kernel,
        out_shape=jax.ShapeDtypeStruct((1, m_dev, half), bf16),
        in_specs=[hbm, smem, vmem, hbm, hbm, hbm, smem, vmem],
        out_specs=hbm,
        scratch_shapes=[
            pltpu.VMEM((n_row, size // n_row, size), f32),
            pltpu.VMEM((size, m_dev), bf16),
            pltpu.VMEM((size, wide), bf16),
            pltpu.VMEM((size, raw_width), bf16),
            pltpu.VMEM((m_dev, half), bf16),
            pltpu.VMEM((m_dev, half), bf16),
            pltpu.VMEM((m_dev, half - raw_width), bf16),
            pltpu.VMEM((size, size), f32),
            pltpu.VMEM((m_dev, size), bf16),
            pltpu.VMEM((m_dev, size), bf16),
            pltpu.VMEM((m_dev, size), bf16),
            pltpu.VMEM((m_dev, size), bf16),
            pltpu.VMEM((block_mask.shape[1], size), f32),
            pltpu.VMEM((block_mask.shape[1], size), f32),
            pltpu.VMEM((m_dev, m_dev), bf16),
            dma((n_row + n_col - 2,)), dma((n_row + n_col - 2,)),
            dma((n_col - 1,)), dma((n_col - 1,)),
            dma((n_row - 1,)), dma((n_row - 1,)),
            dma((n_row - 1,)), dma((n_row - 1,)),
            dma((n_col - 1,)), dma((n_col - 1,)),
            dma((n_z,)), dma((n_z,)),
            dma((5,)),
            dma((len(RAW) + len(COOKED),)),
        ],
        compiler_params=pltpu.CompilerParams(
            collective_id=0, has_side_effects=True, vmem_limit_bytes=48 * 1024 * 1024
        ),
    )(
        diag_block,
        pivot_order,
        pivot_order,
        jnp.swapaxes(lower_in, 1, 2),
        upper_in,
        trailing,
        jnp.swapaxes(block_mask, 1, 2),
        row_map,
    )


def solution(mesh):
    return jax.shard_map(
        local,
        mesh=mesh,
        in_specs=(
            P("cube", ("row", "col"), None),
            P("cube", None),
            P("cube", "row", "col"),
            P("cube", "row", "col"),
            P("cube", "row", "col"),
            P("cube", "row", "col"),
            P("cube", "row"),
        ),
        out_specs=P("cube", "row", "col"),
        check_vma=False,
    )
```

profile of v0, /device:TPU:64, one launch (start us, length us, event | category | flops | bytes accessed | tf_op | source)
XLA Modules:
  0.0 106.2 jit_solution(93071443378472093)
XLA Ops:
  0.0 0.0 copy-start
  0.0 1.0 copy-done
  1.0 0.0 copy-start.1
  1.0 0.8 copy-done.1
  1.9 0.0 copy-start.2
  1.9 0.7 copy-done.2
  2.6 0.0 copy-start.3
  2.6 0.7 copy-done.3
  3.3 0.0 copy-start.4
  3.3 0.7 copy-done.4
  3.9 0.0 copy-start.5
  3.9 0.7 copy-done.5
  4.6 99.7 %shard_map.73 = bf16[1,1024,1920]{2,1,0:T(8,128)(2,1)S(1)} custom-call(f32[1,8,256]{2,1,0:T(8,128)S(1)} %copy-done.2, s32[1,256]{1,0:T(1,128)S(1)} %copy-done.4, s32[1,256]{1,0:T(1,128)S(1)} %copy-done.4, bf16[1,32,1024]{2,1,0:T(8,128)(2,1)S(1)} %bitcast.2, bf16[1,64,3840]{2,1,0:T(8,128)(2,1)S(1)} %copy-done, bf16[1,1024,3840]{2,1,0:T(8,128)(2,1)} %trailing.1, ...), custom_call_target="tpu_custom_call" | custom-call | tf_op jit(solution)/shard_map/pallas_call | solution.py:311
  104.3 1.9 %copy.9 = bf16[1,1024,1920]{2,1,0:T(8,128)(2,1)} copy(bf16[1,1024,1920]{2,1,0:T(8,128)(2,1)S(1)} %shard_map.73) | data formatting | bytes 7864320
Async XLA Ops:
  0.0 1.0 copy-start
  1.0 0.8 copy-start.1
  1.9 0.7 copy-start.2
  2.6 0.7 copy-start.3
  3.3 0.7 copy-start.4
  3.9 0.7 copy-start.5
where the time goes:
time: 107 us; the launch traced here: 106 us
  Pallas kernels  99.7 us (93%)
  local copies, waits for them, and re-layouts  6.53 us (6%)
    pallas_call x1, Pallas kernels, local(): pl.pallas_call(kernel, out_shape=jax.ShapeDtypeStruct((1, m_dev, half), b...  99.7 us
    unnamed x13, local copies, waits for them, and re-layouts  6.53 us

commit v1 on v0

--- a/solution.py
+++ b/solution.py
@@ -8,9 +8,10 @@
 from jax.sharding import PartitionSpec as P
 
 MESH = pl.DeviceIdType.MESH
-RAW = (384, 384, 384)
-COOKED = (384, 256, 128)
+RAW = (512, 384)
+COOKED = (128, 256, 256, 256, 128)
 STEP = 64
+GROUP = 8
 
 
 def offsets(widths, start):
@@ -23,17 +24,30 @@
 
 def invert(amat):
     size = amat.shape[0]
+    narrow = 128
     lane = lax.broadcasted_iota(jnp.int32, (1, size), 1)
     sub = lax.broadcasted_iota(jnp.int32, (STEP, 1), 0)
 
     def block_step(_, carry):
         x = amat[0:STEP, :]
-        for k in range(STEP):
-            column = jnp.broadcast_to(x[:, k : k + 1], (STEP, size))
-            here = lane == k
-            inverse = 1.0 / column[k : k + 1, :]
-            fresh = jnp.where(here, inverse, x[k : k + 1, :] * inverse)
-            x = jnp.where(sub == k, fresh, jnp.where(here, 0.0, x) - column * fresh)
+        for first in range(0, STEP, GROUP):
+            columns = [
+                jnp.broadcast_to(x[:, k : k + 1], (STEP, narrow))
+                for k in range(first, first + GROUP)
+            ]
+            for j in range(GROUP):
+                k = first + j
+                inverse = 1.0 / columns[j][k : k + 1, :]
+                for later in range(j + 1, GROUP):
+                    ratio = columns[later][k : k + 1, :] * inverse
+                    columns[later] = jnp.where(
+                        sub == k, ratio, columns[later] - columns[j] * ratio
+                    )
+                here = lane == k
+                column = jnp.concatenate([columns[j]] * (size // narrow), axis=1)
+                inverse = jnp.concatenate([inverse] * (size // narrow), axis=1)
+                fresh = jnp.where(here, inverse, x[k : k + 1, :] * inverse)
+                x = jnp.where(sub == k, fresh, jnp.where(here, 0.0, x) - column * fresh)
         below = amat[STEP:, :]
         rest = jnp.where(lane < STEP, 0.0, below) - jnp.dot(
             below[:, 0:STEP],
@@ -66,10 +80,10 @@
 
 
 def kernel(
-    diag, order_s, order_v, lower, upper, trailing, mask, row_map, out,
-    dg, lt, u, ug, land, keep, cook, amat, wk, ws, wo, wg, mo, mg, perm,
+    diag, order_in, lower, upper, trailing, mask_in, row_map_in, keep,
+    order_s, order_v, mask, row_map, dg, lt, u, ug, land, cook, amat, wk, ws, wo, wg, mo, mg, perm,
     d_send, d_recv, l_send, l_recv, u_send, u_recv, f_send, f_recv,
-    v_send, v_recv, z_send, z_recv, local_sem, out_sem,
+    v_send, v_recv, z_send, z_recv, local_sem, gate,
 ):
     n_row, n_col = lax.axis_size("row"), lax.axis_size("col")
     c, r, q = lax.axis_index("cube"), lax.axis_index("row"), lax.axis_index("col")
@@ -92,10 +106,31 @@
             device_id=to, device_id_type=MESH,
         )
 
+    small = []
+    for i, (src, dst) in enumerate(
+        [(mask_in, mask), (order_in, order_s), (order_in, order_v), (row_map_in, row_map)]
+    ):
+        copy = pltpu.make_async_copy(src, dst, local_sem.at[5 + i])
+        copy.start()
+        small.append(copy)
+
     barrier = pltpu.get_barrier_semaphore()
-    for mate in [peer] + row_mates + col_mates:
-        pl.semaphore_signal(barrier, inc=1, device_id=mate, device_id_type=MESH)
-    pl.semaphore_wait(barrier, n_row + n_col - 1)
+
+    def signal(semaphore, to):
+        pl.semaphore_signal(semaphore, inc=1, device_id=to, device_id_type=MESH)
+
+    @pl.when(parity == 1)
+    def _():
+        signal(barrier, peer)
+
+    @pl.when(parity == 0)
+    def _():
+        pl.semaphore_wait(barrier, 1)
+        signal(gate, peer)
+
+    @pl.when(parity == 1)
+    def _():
+        pl.semaphore_wait(gate, 1)
 
     d_rows = diag.shape[1]
     d_at = pl.multiple_of(q * d_rows, d_rows)
@@ -106,6 +141,34 @@
     w_rows = m_dev // n_col
     w_at = pl.multiple_of(q * w_rows, w_rows)
 
+    z_copies = []
+
+    def to_peer(src, dst):
+        i = len(z_copies)
+        copy = remote(src, dst, z_send.at[i], z_recv.at[i], peer)
+        copy.start()
+        z_copies.append(copy)
+        return copy
+
+    raw = [
+        to_peer(trailing.at[0, :, pl.ds(sent_at + at, width)], land.at[:, pl.ds(at, width)])
+        for at, width in raw_spans
+    ]
+    u_raw = to_peer(
+        upper.at[0, :, pl.ds(sent_at, raw_width)], ug.at[pl.ds(u_at, u_rows), :]
+    )
+
+    @pl.when(parity == 1)
+    def _():
+        for mate in row_mates + col_mates:
+            signal(barrier, mate)
+        pl.semaphore_wait(barrier, n_row + n_col - 2)
+        signal(gate, peer)
+
+    @pl.when(parity == 0)
+    def _():
+        pl.semaphore_wait(gate, 1)
+
     d_own = pltpu.make_async_copy(diag.at[0], dg.at[r, pl.ds(d_at, d_rows), :], local_sem.at[0])
     d_own.start()
     d_first = []
@@ -114,26 +177,11 @@
         copy.start()
         d_first.append(copy)
 
+    small[0].wait()
     for i in range(mo.shape[0]):
         flag = mask[0, 1 - parity, i].astype(jnp.float32)
         mo[i : i + 1, :] = jnp.full((1, mo.shape[1]), flag, jnp.float32)
-    z_copies = []
-
-    def to_peer(src, dst):
-        i = len(z_copies)
-        copy = remote(src, dst, z_send.at[i], z_recv.at[i], peer)
-        copy.start()
-        z_copies.append(copy)
-        return copy
-
     m_raw = to_peer(mo, mg)
-    u_raw = to_peer(
-        upper.at[0, :, pl.ds(sent_at, raw_width)], ug.at[pl.ds(u_at, u_rows), :]
-    )
-    raw = [
-        to_peer(trailing.at[0, :, pl.ds(sent_at + at, width)], land.at[:, pl.ds(at, width)])
-        for at, width in raw_spans
-    ]
 
     d_own.wait()
     for copy in d_first:
@@ -168,6 +216,8 @@
     )
     keep_in.start()
 
+    for copy in small[1:]:
+        copy.wait()
     tile = 128
     lane = lax.broadcasted_iota(jnp.int32, (tile, tile), 1)
     for i in range(m_dev // tile):
@@ -187,7 +237,7 @@
         amat[pl.ds(i, 1), :] = dg[source // per_row, pl.ds(source % per_row, 1), :]
         return carry
 
-    lax.fori_loop(0, size, pick, 0)
+    lax.fori_loop(0, size, pick, 0, unroll=8)
     invert(amat)
 
     u_raw.wait_recv()
@@ -205,25 +255,32 @@
     low = (left - middle.astype(jnp.float32)).astype(jnp.bfloat16)
     subs = lax.broadcasted_iota(jnp.int32, (size, size), 0)
     hot = jnp.where(subs == order_v[...], 1.0, 0.0).astype(jnp.bfloat16)
+    high, middle, low = [
+        jnp.dot(hot, part, preferred_element_type=jnp.float32).astype(jnp.bfloat16)
+        for part in (high, middle, low)
+    ]
     l_own.wait()
     for copy in l_copies:
         copy.wait_recv()
+    wide = 256
 
     def panel(i, carry):
-        at = pl.multiple_of(i * tile, tile)
-        part = lt[:, pl.ds(at, tile)]
+        part = lt[:, pl.ds(pl.multiple_of(i * wide, wide), wide)]
         wt = (
             jnp.dot(low, part, preferred_element_type=jnp.float32)
             + jnp.dot(middle, part, preferred_element_type=jnp.float32)
             + jnp.dot(high, part, preferred_element_type=jnp.float32)
         )
-        w = jnp.dot(hot, wt.astype(jnp.bfloat16), preferred_element_type=jnp.float32).T
-        wk[pl.ds(at, tile), :] = (w * mask[0, parity, i].astype(jnp.float32)).astype(jnp.bfloat16)
-        ws[pl.ds(at, tile), :] = (w * mask[0, 1 - parity, i].astype(jnp.float32)).astype(jnp.bfloat16)
-        wo[pl.ds(at, tile), :] = w.astype(jnp.bfloat16)
+        w = wt.T
+        for j in range(wide // tile):
+            at = pl.multiple_of(i * wide + j * tile, tile)
+            rows = w[j * tile : (j + 1) * tile, :]
+            flag = mask[0, 1 - parity, i * (wide // tile) + j].astype(jnp.float32)
+            ws[pl.ds(at, tile), :] = (rows * flag).astype(jnp.bfloat16)
+            wo[pl.ds(at, tile), :] = rows.astype(jnp.bfloat16)
         return carry
 
-    lax.fori_loop(0, m_dev // tile, panel, 0)
+    lax.fori_loop(0, m_dev // wide, panel, 0)
     w_raw = to_peer(wo.at[pl.ds(w_at, w_rows), :], wg.at[pl.ds(w_at, w_rows), :])
 
     u_own.wait()
@@ -236,6 +293,10 @@
         update(cook, start, ws, u, sent_at + at, width)
         cooked.append(to_peer(cook.at[:, pl.ds(start, width)], land.at[:, pl.ds(at, width)]))
 
+    for i in range(m_dev // tile):
+        block = slice(i * tile, (i + 1) * tile)
+        flag = mask[0, parity, i].astype(jnp.float32)
+        wk[block, :] = (wo[block, :].astype(jnp.float32) * flag).astype(jnp.bfloat16)
     keep_in.wait()
     for at in range(0, half, 384):
         update(keep, at, wk, u, kept_at + at, 384)
@@ -255,7 +316,7 @@
         ws[block, :] = masked.astype(jnp.bfloat16)
 
     def merge(at, width):
-        rows = 256
+        rows = 512 if width <= tile else 256
 
         def body(step, carry):
             top = pl.multiple_of(step * rows, rows)
@@ -270,30 +331,16 @@
 
         lax.fori_loop(0, m_dev // rows, body, 0)
 
-    outs = []
-
-    def write(at, width):
-        i = len(outs)
-        copy = pltpu.make_async_copy(
-            keep.at[:, pl.ds(at, width)], out.at[0, :, pl.ds(at, width)], out_sem.at[i]
-        )
-        copy.start()
-        outs.append(copy)
-
     for (at, width), copy in zip(raw_spans, raw):
         copy.wait_recv()
         update(land, at, ws, ug, at, width)
         merge(at, width)
-        write(at, width)
     for (at, width), copy in zip(cooked_spans, cooked):
         copy.wait_recv()
         merge(at, width)
-        write(at, width)
 
     for copy in d_first + d_second + l_copies + u_copies + u_pass + w_pass + z_copies:
         copy.wait_send()
-    for copy in outs:
-        copy.wait()
 
 
 def local(diag_block, pivot_order, lower_in, upper_in, trailing, block_mask, row_map):
@@ -305,20 +352,21 @@
     n_z = 3 + len(RAW) + len(COOKED)
     dma = pltpu.SemaphoreType.DMA
     bf16, f32 = jnp.bfloat16, jnp.float32
-    hbm = pl.BlockSpec(memory_space=pl.ANY)
-    vmem = pl.BlockSpec(memory_space=pltpu.VMEM)
-    smem = pl.BlockSpec(memory_space=pltpu.SMEM)
-    return pl.pallas_call(
+    hbm = pl.BlockSpec(memory_space=pltpu.HBM)
+    merged = pl.pallas_call(
         kernel,
-        out_shape=jax.ShapeDtypeStruct((1, m_dev, half), bf16),
-        in_specs=[hbm, smem, vmem, hbm, hbm, hbm, smem, vmem],
-        out_specs=hbm,
+        out_shape=jax.ShapeDtypeStruct((m_dev, half), bf16),
+        in_specs=[hbm] * 7,
+        out_specs=pl.BlockSpec(memory_space=pltpu.VMEM),
         scratch_shapes=[
+            pltpu.SMEM(pivot_order.shape, jnp.int32),
+            pltpu.VMEM(pivot_order.shape, jnp.int32),
+            pltpu.SMEM((1, block_mask.shape[2], block_mask.shape[1]), jnp.int32),
+            pltpu.VMEM(row_map.shape, jnp.int32),
             pltpu.VMEM((n_row, size // n_row, size), f32),
             pltpu.VMEM((size, m_dev), bf16),
             pltpu.VMEM((size, wide), bf16),
             pltpu.VMEM((size, raw_width), bf16),
-            pltpu.VMEM((m_dev, half), bf16),
             pltpu.VMEM((m_dev, half), bf16),
             pltpu.VMEM((m_dev, half - raw_width), bf16),
             pltpu.VMEM((size, size), f32),
@@ -335,22 +383,27 @@
             dma((n_row - 1,)), dma((n_row - 1,)),
             dma((n_col - 1,)), dma((n_col - 1,)),
             dma((n_z,)), dma((n_z,)),
-            dma((5,)),
-            dma((len(RAW) + len(COOKED),)),
+            dma((9,)),
+            pltpu.SemaphoreType.REGULAR,
         ],
         compiler_params=pltpu.CompilerParams(
             collective_id=0, has_side_effects=True, vmem_limit_bytes=48 * 1024 * 1024
         ),
     )(
-        diag_block,
-        pivot_order,
-        pivot_order,
-        jnp.swapaxes(lower_in, 1, 2),
-        upper_in,
-        trailing,
-        jnp.swapaxes(block_mask, 1, 2),
-        row_map,
+        *[
+            pltpu.with_memory_space_constraint(item, pltpu.HBM)
+            for item in (
+                diag_block,
+                pivot_order,
+                jnp.swapaxes(lower_in, 1, 2),
+                upper_in,
+                trailing,
+                jnp.swapaxes(block_mask, 1, 2),
+                row_map,
+            )
+        ]
     )
+    return merged[None]
 
 
 def solution(mesh):

time: 107 us -> 98.1 us (0.917)
  local copies, waits for them, and re-layouts: 6.53 us -> 1.93 us
  Pallas kernels: 99.7 us -> 96.1 us
    unnamed x13 -> x1, local copies, waits for them, and re-layouts: 6.53 us -> 1.93 us
    pallas_call x1, Pallas kernels: 99.7 us -> 96.1 us  [local(): pl.pallas_call(kernel, out_shape=jax.ShapeDtypeStruct((m_dev, half), bf16...]
where the time goes in v1:
time: 98.1 us; the launch traced here: 98 us
  Pallas kernels  96.1 us (98%)
  local copies, waits for them, and re-layouts  1.93 us (2%)
    pallas_call x1, Pallas kernels, local(): pl.pallas_call(kernel, out_shape=jax.ShapeDtypeStruct((m_dev, half), bf16...  96.1 us

profile of v1, /device:TPU:64, one launch (start us, length us, event | category | flops | bytes accessed | tf_op | source)
XLA Modules:
  0.0 98.0 jit_solution(3016639896083143531)
XLA Ops:
  0.0 96.1 %shard_map.73 = bf16[1024,1920]{1,0:T(8,128)(2,1)S(1)} custom-call(f32[1,8,256]{2,1,0:T(8,128)} %diag.1, s32[1,256]{1,0:T(1,128)} %order_in.1, bf16[1,32,1024]{2,1,0:T(8,128)(2,1)} %bitcast.4, bf16[1,64,3840]{2,1,0:T(8,128)(2,1)} %upper.1, bf16[1,1024,3840]{2,1,0:T(8,128)(2,1)} %trailing.1, s32[1,2,8]{2,1,0:T(2,128)} %bitcast.5, s32[1,1024]{1,0:T(1,128)} %row_map_in.1), custom_call_target="tpu_custom_call" | custom-call | tf_op jit(solution)/shard_map/pallas_call | solution.py:356
  96.1 1.9 %copy.9 = bf16[1,1024,1920]{2,1,0:T(8,128)(2,1)} copy(bf16[1,1024,1920]{2,1,0:T(8,128)(2,1)S(1)} %bitcast.3) | data formatting | bytes 7864320

commit v2 on v1

--- a/solution.py
+++ b/solution.py
@@ -8,8 +8,8 @@
 from jax.sharding import PartitionSpec as P
 
 MESH = pl.DeviceIdType.MESH
-RAW = (512, 384)
-COOKED = (128, 256, 256, 256, 128)
+RAW = (384, 256)
+COOKED = (128, 256, 384, 384, 128)
 STEP = 64
 GROUP = 8
 
@@ -81,7 +81,7 @@
 
 def kernel(
     diag, order_in, lower, upper, trailing, mask_in, row_map_in, keep,
-    order_s, order_v, mask, row_map, dg, lt, u, ug, land, cook, amat, wk, ws, wo, wg, mo, mg, perm,
+    order_s, order_v, mask, row_map, dg, lt, u, ug, land, cook, amat, wk, ws, wo, wg, mo, mg, part_sum, perm,
     d_send, d_recv, l_send, l_recv, u_send, u_recv, f_send, f_recv,
     v_send, v_recv, z_send, z_recv, local_sem, gate,
 ):
@@ -193,6 +193,20 @@
         copy.start()
         d_second.append(copy)
 
+    def spread(at, width, turn):
+        src = upper.at[0, :, pl.ds(at, width)]
+        dst = u.at[pl.ds(u_at, u_rows), pl.ds(at, width)]
+        own = pltpu.make_async_copy(src, dst, local_sem.at[2 + 7 * turn])
+        own.start()
+        away = []
+        for i, mate in enumerate(row_mates):
+            sem = turn * (n_row - 1) + i
+            copy = remote(src, dst, u_send.at[sem], u_recv.at[sem], mate)
+            copy.start()
+            away.append(copy)
+        return own, away
+
+    u_cook = spread(sent_at + raw_width, half - raw_width, 0)
     l_own = pltpu.make_async_copy(lower.at[0], lt.at[pl.ds(l_at, l_rows), :], local_sem.at[1])
     l_own.start()
     l_copies = []
@@ -200,13 +214,7 @@
         copy = remote(lower.at[0], lt.at[pl.ds(l_at, l_rows), :], l_send.at[i], l_recv.at[i], mate)
         copy.start()
         l_copies.append(copy)
-    u_own = pltpu.make_async_copy(upper.at[0], u.at[pl.ds(u_at, u_rows), :], local_sem.at[2])
-    u_own.start()
-    u_copies = []
-    for i, mate in enumerate(row_mates):
-        copy = remote(upper.at[0], u.at[pl.ds(u_at, u_rows), :], u_send.at[i], u_recv.at[i], mate)
-        copy.start()
-        u_copies.append(copy)
+    u_kept = spread(kept_at, half, 1)
     cook_in = pltpu.make_async_copy(
         trailing.at[0, :, pl.ds(sent_at + raw_width, half - raw_width)], cook, local_sem.at[3]
     )
@@ -283,21 +291,34 @@
     lax.fori_loop(0, m_dev // wide, panel, 0)
     w_raw = to_peer(wo.at[pl.ds(w_at, w_rows), :], wg.at[pl.ds(w_at, w_rows), :])
 
-    u_own.wait()
-    for copy in u_copies:
+    u_cook[0].wait()
+    for copy in u_cook[1]:
         copy.wait_recv()
     cook_in.wait()
     cooked = []
     for at, width in cooked_spans:
         start = at - raw_width
         update(cook, start, ws, u, sent_at + at, width)
-        cooked.append(to_peer(cook.at[:, pl.ds(start, width)], land.at[:, pl.ds(at, width)]))
+        if at + width < half:
+            cooked.append(to_peer(cook.at[:, pl.ds(start, width)], land.at[:, pl.ds(at, width)]))
+    last_at, last = cooked_spans[-1]
+    upper_half = m_dev // 2
+    tail = [
+        to_peer(
+            cook.at[pl.ds(top, upper_half), pl.ds(last_at - raw_width, last)],
+            land.at[pl.ds(top, upper_half), pl.ds(last_at, last)],
+        )
+        for top in (0, upper_half)
+    ]
 
     for i in range(m_dev // tile):
         block = slice(i * tile, (i + 1) * tile)
         flag = mask[0, parity, i].astype(jnp.float32)
         wk[block, :] = (wo[block, :].astype(jnp.float32) * flag).astype(jnp.bfloat16)
     keep_in.wait()
+    u_kept[0].wait()
+    for copy in u_kept[1]:
+        copy.wait_recv()
     for at in range(0, half, 384):
         update(keep, at, wk, u, kept_at + at, 384)
 
@@ -312,7 +333,8 @@
         copy.wait_recv()
     for i in range(mg.shape[0]):
         block = slice(i * tile, (i + 1) * tile)
-        masked = wg[block, :].astype(jnp.float32) * mg[i : i + 1, :]
+        flag = jnp.concatenate([mg[i : i + 1, :]] * (size // tile), axis=1)
+        masked = wg[block, :].astype(jnp.float32) * flag
         ws[block, :] = masked.astype(jnp.bfloat16)
 
     def merge(at, width):
@@ -339,7 +361,26 @@
         copy.wait_recv()
         merge(at, width)
 
-    for copy in d_first + d_second + l_copies + u_copies + u_pass + w_pass + z_copies:
+    tail[0].wait_recv()
+    for top in range(0, m_dev, upper_half):
+        rows = slice(top, top + upper_half)
+        part_sum[rows, :] = jnp.dot(
+            perm[rows, :upper_half],
+            land[:upper_half, last_at:],
+            preferred_element_type=jnp.float32,
+        )
+    tail[1].wait_recv()
+    for top in range(0, m_dev, upper_half):
+        rows = slice(top, top + upper_half)
+        taken = part_sum[rows, :] + jnp.dot(
+            perm[rows, upper_half:],
+            land[upper_half:, last_at:],
+            preferred_element_type=jnp.float32,
+        )
+        total = keep[rows, last_at:].astype(jnp.float32) + taken
+        keep[rows, last_at:] = total.astype(jnp.bfloat16)
+
+    for copy in d_first + d_second + l_copies + u_cook[1] + u_kept[1] + u_pass + w_pass + z_copies:
         copy.wait_send()
 
 
@@ -349,7 +390,7 @@
     m_dev, wide = trailing.shape[1:]
     half = wide // 2
     raw_width = sum(RAW)
-    n_z = 3 + len(RAW) + len(COOKED)
+    n_z = 4 + len(RAW) + len(COOKED)
     dma = pltpu.SemaphoreType.DMA
     bf16, f32 = jnp.bfloat16, jnp.float32
     hbm = pl.BlockSpec(memory_space=pltpu.HBM)
@@ -374,16 +415,17 @@
             pltpu.VMEM((m_dev, size), bf16),
             pltpu.VMEM((m_dev, size), bf16),
             pltpu.VMEM((m_dev, size), bf16),
-            pltpu.VMEM((block_mask.shape[1], size), f32),
-            pltpu.VMEM((block_mask.shape[1], size), f32),
+            pltpu.VMEM((block_mask.shape[1], 128), f32),
+            pltpu.VMEM((block_mask.shape[1], 128), f32),
+            pltpu.VMEM((m_dev, 128), f32),
             pltpu.VMEM((m_dev, m_dev), bf16),
             dma((n_row + n_col - 2,)), dma((n_row + n_col - 2,)),
             dma((n_col - 1,)), dma((n_col - 1,)),
-            dma((n_row - 1,)), dma((n_row - 1,)),
+            dma((2 * n_row - 2,)), dma((2 * n_row - 2,)),
             dma((n_row - 1,)), dma((n_row - 1,)),
             dma((n_col - 1,)), dma((n_col - 1,)),
             dma((n_z,)), dma((n_z,)),
-            dma((9,)),
+            dma((10,)),
             pltpu.SemaphoreType.REGULAR,
         ],
         compiler_params=pltpu.CompilerParams(

time: 98.1 us -> 97.1 us (0.990)
  Pallas kernels: 96.1 us -> 95 us
    pallas_call x1, Pallas kernels: 96.1 us -> 95 us  [local(): pl.pallas_call(kernel, out_shape=jax.ShapeDtypeStruct((m_dev, half), bf16...]
where the time goes in v2:
time: 97.1 us; the launch traced here: 97 us
  Pallas kernels  95 us (98%)
  local copies, waits for them, and re-layouts  1.93 us (2%)
    pallas_call x1, Pallas kernels, local(): pl.pallas_call(kernel, out_shape=jax.ShapeDtypeStruct((m_dev, half), bf16...  95 us

profile of v2, /device:TPU:64, one launch (start us, length us, event | category | flops | bytes accessed | tf_op | source)
XLA Modules:
  0.0 97.0 jit_solution(10267605798259504798)
XLA Ops:
  0.0 95.0 %shard_map.73 = bf16[1024,1920]{1,0:T(8,128)(2,1)S(1)} custom-call(f32[1,8,256]{2,1,0:T(8,128)} %diag.1, s32[1,256]{1,0:T(1,128)} %order_in.1, bf16[1,32,1024]{2,1,0:T(8,128)(2,1)} %bitcast.4, bf16[1,64,3840]{2,1,0:T(8,128)(2,1)} %upper.1, bf16[1,1024,3840]{2,1,0:T(8,128)(2,1)} %trailing.1, s32[1,2,8]{2,1,0:T(2,128)} %bitcast.5, s32[1,1024]{1,0:T(1,128)} %row_map_in.1), custom_call_target="tpu_custom_call" | custom-call | tf_op jit(solution)/shard_map/pallas_call | solution.py:397
  95.0 1.9 %copy.9 = bf16[1,1024,1920]{2,1,0:T(8,128)(2,1)} copy(bf16[1,1024,1920]{2,1,0:T(8,128)(2,1)S(1)} %bitcast.3) | data formatting | bytes 7864320
